TPU v7x, 32 devices: a whole 2x2x4 slice. The times are simulated.
32 devices in a mesh: groups: 2 (over x), seq: 8 (over z, y), segment: 2 (over core).
Axes of the slice: x: 2, y: 2, z: 4, core: 2. Of those that a mesh axis runs over, the one named last changes fastest.
Arguments:
- queue_frames: bfloat16 [32, 32, 5120], P(('groups', 'segment'), 'seq'), parts along dimension 0, may hold values from -450 to 450
- fresh_frames: bfloat16 [2, 32, 5120], P('groups', 'seq'), parts along dimension 0, may hold values from -450 to 450
- slot_level: int32 [32], P(('groups', 'segment')), parts along dimension 0, may hold values from 0 to 49
- window_start: int32 [32], P(('groups', 'segment')), parts along dimension 0, may hold values from 0 to 3
- shift_table: float32 [50, 5120], replicated, may hold values from -3 to 3
- scale_table: float32 [50, 5120], replicated, may hold values from -1.5 to 1.5
- gate_table: float32 [50, 5120], replicated, may hold values from -10 to 10
- w_query: bfloat16 [5120, 4096], P(None, 'seq'), may hold values from -3.5 to 3.5
- w_key: bfloat16 [5120, 4096], P(None, 'seq'), may hold values from -3.5 to 3.5
- w_value: bfloat16 [5120, 4096], P(None, 'seq'), may hold values from -0.078125 to 0.078125
- w_out: bfloat16 [4096, 5120], P('seq'), may hold values from -0.5 to 0.5
- query_gain: float32 [4096], P('seq'), may hold values from 0.1 to 1.9
- key_gain: float32 [4096], P('seq'), may hold values from 0.1 to 1.9
Outputs:
- queue_out: bfloat16 [32, 32, 5120], P(('groups', 'segment'), 'seq'), parts along dimension 0
- departed: bfloat16 [4, 1, 32, 5120], P(('groups', 'segment'), None, 'seq'), parts along dimension 0
There are 2 independent parts, one for each index of `groups`. A program takes and returns all parts, laid end to end along the dimension named above; an argument that names none is the same for every part. Nothing has to cross between parts.
All inputs are finite; a program needn't handle non-finite values.
Results may differ from a plain program's by a relative error of at most 0.02.
Values may be sent and summed in bfloat16 or wider, within the bound.
A program may use at most 128 MiB of HBM per device.

v0:
```python
import jax
import jax.numpy as jnp
from jax import lax
from jax.sharding import PartitionSpec as P

HD = 128
HEADS = 32
KEYWIN = 4


epsilon = 1e-06
masked_score = -1e30


def from_behind(block, axis, distance):
    devices = range(lax.axis_size(axis))
    route = [(i - distance, i) for i in devices if i - distance in devices]
    return lax.ppermute(block, axis, route)


def extended(x, sides, width):
    for axis, dim in sides:
        peers, length = (lax.axis_size(axis), x.shape[dim])
        up = [(i, (i + 1) % peers) for i in range(peers - 1)]
        down = [(j, i) for i, j in up]
        last = lax.slice_in_dim(x, length - width, length, axis=dim)
        leading = lax.slice_in_dim(x, 0, width, axis=dim)
        before = lax.ppermute(last, axis, up)
        after = lax.ppermute(leading, axis, down)
        x = jnp.concatenate([before, x, after], axis=dim)
    return x


def modulate(level_ids, lookup):
    onehot = (level_ids[:, None] == jnp.arange(lookup.shape[0], dtype=jnp.int32)[None, :]).astype(
        jnp.float32
    )
    return jnp.dot(onehot, lookup, precision=lax.Precision.HIGHEST)


def scaled(raw, total_squares, gain):
    inverse = lax.rsqrt(total_squares / (HEADS * HD) + epsilon)
    return (raw * inverse[:, :, None] * gain).astype(jnp.bfloat16)


def attend(queries, keys, value_rows, window_start, segment_idx, queue_len):
    rim_width = KEYWIN - 1
    frames = queries.shape[0]
    token_count = queries.shape[1]
    local_width = queries.shape[2]
    heads_local = local_width // HD
    begins = jnp.arange(frames, dtype=jnp.int32) + rim_width - window_start

    def window(source):

        def take(begin):
            return lax.dynamic_slice_in_dim(source, begin, KEYWIN, 0)

        return jax.vmap(take)(begins).reshape(frames, KEYWIN * token_count, heads_local, HD)

    key_rows = window(keys)
    value_win = window(value_rows)
    frame_ids = (
        segment_idx * frames
        + begins[:, None]
        - rim_width
        + jnp.arange(KEYWIN, dtype=jnp.int32)[None, :]
    )
    usable = jnp.repeat((frame_ids >= 0) & (frame_ids < queue_len), token_count, axis=1)
    query_heads = queries.reshape(frames, token_count, heads_local, HD)
    scores = jnp.einsum(
        "fqhd,fkhd->fhqk", query_heads, key_rows, preferred_element_type=jnp.float32
    ) * HD ** (-0.5)
    scores = jnp.where(usable[:, None, None, :], scores, masked_score)
    largest = jnp.max(scores, axis=3, keepdims=True)
    lifted = jnp.exp(scores - largest)
    totals = jnp.sum(lifted, axis=3, keepdims=True)
    weights = (lifted / totals).astype(jnp.bfloat16)
    outputs = jnp.einsum("fhqk,fkhd->qfhd", weights, value_win, preferred_element_type=jnp.float32)
    return outputs.astype(jnp.bfloat16).reshape(token_count, frames, local_width)


def handoff(updated, incoming):
    handed = from_behind(updated[0], "segment", -1)
    last_segment = lax.axis_index("segment") == lax.axis_size("segment") - 1
    arriving = jnp.where(last_segment, incoming, handed)
    return jnp.concatenate([updated[1:], arriving[None]], axis=0)


def shards(
    queue_frames,
    fresh_frames,
    slot_level,
    window_start,
    shift_table,
    scale_table,
    gate_table,
    w_query,
    w_key,
    w_value,
    w_out,
    query_gain,
    key_gain,
):
    segment_idx = lax.axis_index("segment")
    frames = queue_frames.shape[0]
    queue_len = frames * lax.axis_size("segment")
    rim_width = KEYWIN - 1
    local_width = w_query.shape[1]
    w_joined = jnp.concatenate([w_query, w_key, w_value], axis=1)
    shift_rows = modulate(slot_level, shift_table)
    scale_rows = modulate(slot_level, scale_table)
    gate_rows = modulate(slot_level, gate_table)
    queue_state = queue_frames
    values_in = queue_state.astype(jnp.float32)
    inverse = lax.rsqrt(jnp.mean(values_in * values_in, axis=2) + epsilon)
    hidden = (
        values_in * inverse[:, :, None] * (1.0 + scale_rows[:, None]) + shift_rows[:, None]
    ).astype(jnp.bfloat16)
    joined = jnp.einsum(
        "ftd,de->fte",
        lax.all_gather(hidden, "seq", axis=1, tiled=True),
        w_joined,
        preferred_element_type=jnp.float32,
    )
    q_raw = joined[:, :, :local_width]
    k_raw = joined[:, :, local_width : 2 * local_width]
    own_values = joined[:, :, 2 * local_width :].astype(jnp.bfloat16)
    q_squares, k_squares = lax.psum(
        (jnp.sum(q_raw * q_raw, axis=2), jnp.sum(k_raw * k_raw, axis=2)), "seq"
    )
    queries = scaled(q_raw, q_squares, query_gain)
    own_keys = scaled(k_raw, k_squares, key_gain)
    paired = extended(jnp.stack([own_keys, own_values]), (("segment", 1),), rim_width)
    keys = paired[0]
    value_rows = paired[1]
    attended = attend(queries, keys, value_rows, window_start, segment_idx, queue_len)
    partial_value = jnp.einsum(
        "tfe,ed->tfd", attended, w_out, preferred_element_type=jnp.float32
    ).astype(jnp.bfloat16)
    partial_value = lax.optimization_barrier(partial_value)
    summed = lax.psum_scatter(
        partial_value.astype(jnp.float32).astype(jnp.bfloat16),
        "seq",
        scatter_dimension=0,
        tiled=True,
    ).astype(jnp.float32)
    projected = jnp.transpose(summed, (1, 0, 2))
    updated = (values_in + gate_rows[:, None] * projected).astype(jnp.bfloat16)
    departed = [updated[0]]
    queue_state = handoff(updated, fresh_frames[0])
    return (queue_state, jnp.stack(departed)[None])


def solution(mesh):
    return jax.shard_map(
        shards,
        mesh=mesh,
        in_specs=(
            P(("groups", "segment"), "seq", None),
            P("groups", "seq", None),
            P(("groups", "segment")),
            P(("groups", "segment")),
            P(),
            P(),
            P(),
            P(None, "seq"),
            P(None, "seq"),
            P(None, "seq"),
            P("seq", None),
            P("seq"),
            P("seq"),
        ),
        out_specs=(
            P(("groups", "segment"), "seq", None),
            P(("groups", "segment"), None, "seq", None),
        ),
        check_vma=False,
    )
```

profile of v0, /device:TPU:0, one launch (start us, length us, event | category | flops | bytes accessed | tf_op | source)
XLA Modules:
  0.0 200.0 jit_solution(8836512309598153663)
XLA Ops:
  7.2 0.0 copy-start
  7.2 0.0 all-gather.2.cloned.1.call-start
  7.2 1.2 copy-done
  8.4 1.1 convolution_add_fusion
  9.6 1.7 fusion.26
  11.3 1.2 fusion.10
  12.6 1.9 fusion.13
  14.5 0.0 all-gather.2.cloned.1.call-update
  14.5 0.0 reduce-scatter.2.cloned.1.call-start
  14.5 0.7 add_add_fusion
  15.2 56.8 %all-gather.2.cloned.1.call-done = bf16[8,32,5120]{2,0,1:T(8,128)(2,1)} async-done(((bf16[8,4,5120]{2,0,1:T(8,128)(2,1)}), bf16[8,32,5120]{2,0,1:T(8,128)(2,1)}) %all-gather.2.cloned.1.call-update) | async-done | bytes 2621456 | tf_op jit(solution)/shard_map/all_gather | solution.py:122
  72.0 8.6 %fusion.1 = f32[8,32,1536]{2,1,0:T(8,128)S(1)} fusion(bf16[5120,512]{1,0:T(8,128)(2,1)} %param.22, bf16[5120,512]{1,0:T(8,128)(2,1)} %param.21, bf16[5120,512]{1,0:T(8,128)(2,1)} %param.20, bf16[8,32,5120]{2,0,1:T(8,128)(2,1)} %all-gather.2.cloned.1.call-done), kind=kOutput, calls=%fused_computation.4 | convolution fusion | flops 4073717760 | bytes 19922944 | tf_op jit(solution)/shard_map/ftd,de->fte/dot_general | solution.py:120
  80.6 0.1 multiply_reduce_fusion
  80.8 19.3 %all-reduce.1 = (f32[8,32]{1,0:T(8,128)S(1)}, f32[8,32]{1,0:T(8,128)S(1)}) all-reduce(f32[8,32]{1,0:T(8,128)S(1)} %get-tuple-element.7, f32[8,32]{1,0:T(8,128)S(1)} %get-tuple-element.6), channel_id=1, replica_groups=mesh['groups'=2,'seq'=8,'segment'=2] {'seq'}, use_global_device_ids=true, to_apply=%region_2.0 | all-reduce | flops 512 | bytes 4096 | tf_op jit(solution)/shard_map/psum | solution.py:129
  100.0 0.0 copy-done.6
  100.1 0.0 copy-done.7
  100.1 0.2 fusion.16
  100.3 1.3 collective-permute-start
  101.6 1.3 collective-permute-start.1
  102.9 0.1 fusion.28
  103.0 0.1 broadcast_in_dim.17
  103.0 0.1 broadcast_in_dim.18
  103.1 0.0 collective-permute-done
  103.1 1.8 collective-permute-done.1
  104.9 0.1 pad_maximum_fusion
  105.1 0.1 slice_bitcast_fusion.1
  105.1 1.6 gather_fusion.1
  106.7 1.3 reshape.38
  108.1 0.6 fusion.5
  108.7 0.4 fusion.36
  109.1 0.6 gather_fusion
  109.7 1.1 reshape.36
  110.9 3.0 %fusion.7 = bf16[32,8,4,128]{3,0,2,1:T(8,128)(2,1)S(1)} fusion(bf16[8,128,4,128]{3,2,1,0:T(4,128)(2,1)} %reshape.36, f32[8,4,32]{2,1,0:T(4,128)S(1)} %fusion.36, f32[8,4,32,128]{3,2,1,0:T(8,128)S(1)} %fusion.5), kind=kOutput, calls=%fused_computation.14 | convolution fusion | flops 34079872 | bytes 1839104 | tf_op jit(solution)/shard_map/fhqk,fkhd->qfhd/dot_general | solution.py:79
  113.9 0.0 copy-start.5
  113.9 0.0 copy-start.1
  113.9 0.0 copy-start.3
  113.9 5.7 %convolution_convert_fusion = bf16[32,8,5120]{2,1,0:T(8,128)(2,1)} fusion(bf16[512,5120]{1,0:T(8,128)(2,1)} %param.23, bf16[32,8,4,128]{3,0,2,1:T(8,128)(2,1)S(1)} %fusion.7), kind=kOutput, calls=%fused_computation.5 | convolution fusion | flops 1343488000 | bytes 8126464 | tf_op jit(solution)/shard_map/tfe,ed->tfd/dot_general | solution.py:138
  119.6 0.0 reduce-scatter.2.cloned.1.call-update
  119.7 0.5 fusion.27
  120.2 67.5 %reduce-scatter.2.cloned.1.call-done = bf16[4,8,5120]{2,1,0:T(8,128)(2,1)} async-done(((bf16[32,8,5120]{2,1,0:T(8,128)(2,1)}), bf16[4,8,5120]{2,1,0:T(8,128)(2,1)}) %reduce-scatter.2.cloned.1.call-update) | async-done | bytes 327696 | tf_op jit(solution)/shard_map/reduce_scatter | solution.py:142
  187.6 1.1 fusion.14
  188.8 0.0 copy-start.4
  188.8 1.3 collective-permute-start.2
  190.1 0.1 slice.49
  190.2 1.7 collective-permute-done.2
  192.0 0.1 copy.38
  192.0 0.2 pad_maximum_fusion.1
  192.2 1.0 copy.39
  (15 shorter events, 0.2 us)
Async XLA Ops:
  7.2 1.3 copy-start
  7.2 64.8 %all-gather.2.cloned.1.call-start = ((), (), s32[]{:S(2)}) async-start(), calls=%async_computation.1 | async-start | bytes 2949120 | tf_op jit(solution)/shard_map/all_gather | solution.py:122
  14.5 173.2 %reduce-scatter.2.cloned.1.call-start = ((), (), s32[]{:S(2)}) async-start(), calls=%async_computation.2 | async-start | bytes 2949120 | tf_op jit(solution)/shard_map/reduce_scatter | solution.py:142
  15.2 84.8 %copy-start.6 = (f32[512]{0:T(512)S(1)}, f32[512]{0:T(512)}, u32[]{:S(2)}) copy-start(f32[512]{0:T(512)} %param.24) | copy-start | bytes 6148
  15.2 84.9 %copy-start.7 = (f32[512]{0:T(512)S(1)}, f32[512]{0:T(512)}, u32[]{:S(2)}) copy-start(f32[512]{0:T(512)} %param.25) | copy-start | bytes 6148
  100.3 2.9 %collective-permute-start = (bf16[2,3,32,512]{3,2,1,0:T(8,128)(2,1)S(1)}, bf16[2,3,32,512]{3,2,1,0:T(8,128)(2,1)S(1)}, u32[]{:S(2)}, u32[]{:S(2)}) collective-permute-start(bf16[2,3,32,512]{3,2,1,0:T(8,128)(2,1)S(1)} %get-tuple-element.14), channel_id=1, source_target_pairs={{0,1},{2,3},{4,5},{6,7},{8,9},{10,11},{12,13},{14,15},{16,17},{18,... | collective-permute-start | bytes 589832 | tf_op jit(solution)/shard_map/ppermute | solution.py:28
  101.6 3.3 %collective-permute-start.1 = (bf16[2,3,32,512]{3,2,1,0:T(8,128)(2,1)S(1)}, bf16[2,3,32,512]{3,2,1,0:T(8,128)(2,1)S(1)}, u32[]{:S(2)}, u32[]{:S(2)}) collective-permute-start(bf16[2,3,32,512]{3,2,1,0:T(8,128)(2,1)S(1)} %get-tuple-element.15), channel_id=1, source_target_pairs={{1,0},{3,2},{5,4},{7,6},{9,8},{11,10},{13,12},{15,14},{17,16},{19,... | collective-permute-start | bytes 589832 | tf_op jit(solution)/shard_map/ppermute | solution.py:29
  113.9 5.8 %copy-start.2 = (f32[50,5120]{1,0:T(8,128)S(1)}, f32[50,5120]{1,0:T(8,128)}, u32[]{:S(2)}) copy-start(f32[50,5120]{1,0:T(8,128)} %param.19) | copy-start | bytes 3072004
  113.9 5.8 %copy-start.5 = (s32[8]{0:T(128)S(1)}, s32[8]{0:T(128)}, u32[]{:S(2)}) copy-start(s32[8]{0:T(128)} %param.15) | copy-start | bytes 100
  113.9 73.7 %copy-start.1 = (bf16[8,4,5120]{2,1,0:T(4,128)(2,1)S(1)}, bf16[8,4,5120]{2,1,0:T(4,128)(2,1)}, u32[]{:S(2)}) copy-start(bf16[8,4,5120]{2,1,0:T(4,128)(2,1)} %param.13) | copy-start | bytes 983044
  113.9 78.0 %copy-start.3 = (bf16[1,4,5120]{2,1,0:T(4,128)(2,1)S(1)}, bf16[1,4,5120]{2,1,0:T(4,128)(2,1)}, u32[]{:S(2)}) copy-start(bf16[1,4,5120]{2,1,0:T(4,128)(2,1)} %param.14) | copy-start | bytes 122884
  188.8 4.4 %copy-start.4 = (bf16[1,4,5120]{2,1,0:T(4,128)(2,1)}, bf16[1,4,5120]{2,1,0:T(4,128)(2,1)S(1)}, u32[]{:S(2)}) copy-start(bf16[1,4,5120]{2,1,0:T(4,128)(2,1)S(1)} %copy.62) | copy-start | bytes 122884
  188.8 3.1 %collective-permute-start.2 = (bf16[4,5120]{1,0:T(4,128)(2,1)S(1)}, bf16[4,5120]{1,0:T(4,128)(2,1)S(1)}, u32[]{:S(2)}, u32[]{:S(2)}) collective-permute-start(bf16[4,5120]{1,0:T(4,128)(2,1)S(1)} %bitcast.46), channel_id=1, source_target_pairs={{1,0},{3,2},{5,4},{7,6},{9,8},{11,10},{13,12},{15,14},{17,16},{19,... | collective-permute-start | bytes 122888 | tf_op jit(solution)/shard_map/ppermute | solution.py:18
Sparse Core Ops, SparseCore 0:
  14.6 57.3 all-gather.1
  119.8 67.7 reduce-scatter.1
where the time goes:
time: 200 us
  waiting for transfers between devices  128 us (64%)
  matrix products  21.3 us (11%)
  blocking collectives  19.3 us (10%)
  between operations  14.3 us (7%)
  local copies, waits for them, and re-layouts  7.4 us (4%)
  other arithmetic  6.01 us (3%)
  starting transfers between devices  3.97 us (2%)
    reduce_scatter x1, waiting for transfers between devices, shards(): lax.psum_scatter(partial_value.astype(jnp.float32).astype(jnp.bfloat16),...  67.5 us
    all_gather x1, waiting for transfers between devices, shards(): lax.all_gather(hidden, 'seq', axis=1, tiled=True)  56.8 us
    psum x1, blocking collectives, shards(): lax.psum((jnp.sum(q_raw * q_raw, axis=2), jnp.sum(k_raw * k_raw, axis=2))...  19.3 us
    dot_general x1, matrix products, shards(): jnp.einsum('ftd,de->fte', lax.all_gather(hidden, 'seq', axis=1, tiled=Tru...  8.56 us
    dot_general x1, matrix products, shards(): jnp.einsum('tfe,ed->tfd', attended, w_out, preferred_element_type=jnp.flo...  5.7 us
  transfers between devices with their start and end apart: 5, of which 4 were waited for; matrix products, arithmetic and copies ran while one was open for 1% of the time, Pallas kernels for 0%

commit v1 on v0

v1 whole, which is shorter than its diff:
```python
import functools

import jax
import jax.numpy as jnp
from jax import lax
from jax.experimental import pallas as pl
from jax.experimental.pallas import tpu as pltpu
from jax.sharding import PartitionSpec as P

HD = 128
KEYWIN = 4
epsilon = 1e-06
masked_score = -1e30
MESH = pl.DeviceIdType.MESH
F32 = jnp.float32
BF16 = jnp.bfloat16
NT = (((1,), (1,)), ((), ()))


def quotient(x, n):
    return x >> (n.bit_length() - 1) if n & (n - 1) == 0 else x // n


def remainder(x, n):
    return x & (n - 1) if n & (n - 1) == 0 else x % n


def chunk_count(width):
    lanes = width // 128
    return max(k for k in range(1, 9) if lanes % k == 0)


def kernel(
    n, frames, tok, parts,
    x_ref, fresh_ref, level_ref, start_ref, shift_hbm, scale_hbm, gate_hbm,
    wq_hbm, wk_hbm, wv_hbm, wo_hbm, qgain_ref, kgain_ref,
    queue_ref, departed_ref,
    shift_rows, scale_rows, gate_rows, w_in, w_out, hidden, gathered, raw, stats, keys, vals, att,
    partial, from_y, from_up, from_down, projected, hand,
    local_sem, wo_sem, ag_send, ag_recv, st_send, st_recv, kv_send, kv_recv,
    y_send, y_recv, z_send, up_recv, down_recv, hand_send, hand_recv,
):
    me = lax.axis_index("seq")
    seg = lax.axis_index("segment")
    other = 1 - seg
    nz = n // 2
    z, y = quotient(me, 2), remainder(me, 2)
    block = frames * tok
    rows = n * block
    width = x_ref.shape[2]
    cw = width // parts
    lw = qgain_ref.shape[1]
    heads = lw // HD

    def local(k, src, dst):
        return pltpu.make_async_copy(src, dst, local_sem.at[k])

    locals_ = [
        local(0, shift_hbm, shift_rows),
        local(1, scale_hbm, scale_rows),
        local(2, wq_hbm, w_in.at[:, pl.ds(0, lw)]),
        local(3, wk_hbm, w_in.at[:, pl.ds(lw, lw)]),
        local(4, wv_hbm, w_in.at[:, pl.ds(2 * lw, lw)]),
        local(5, gate_hbm, gate_rows),
    ]
    wo_copies = [
        pltpu.make_async_copy(wo_hbm.at[:, pl.ds(c * cw, cw)], w_out.at[c], wo_sem.at[c])
        for c in range(parts)
    ]
    for copy in locals_ + wo_copies:
        copy.start()

    def remote(src, dst, send, recv, s, g):
        return pltpu.make_async_remote_copy(
            src_ref=src, dst_ref=dst, send_sem=send, recv_sem=recv,
            device_id={"seq": s, "segment": g}, device_id_type=MESH,
        )

    barrier = pltpu.get_barrier_semaphore()

    @pl.loop(1, 2 * n)
    def _(k):
        peer = remainder(me * 2 + seg + k, 2 * n)
        pl.semaphore_signal(
            barrier, inc=1,
            device_id={"seq": quotient(peer, 2), "segment": remainder(peer, 2)},
            device_id_type=MESH,
        )

    locals_[0].wait()
    locals_[1].wait()
    for f in range(frames):
        level = level_ref[f]
        x = x_ref[f].astype(F32)
        inverse = lax.rsqrt(jnp.mean(x * x, axis=1, keepdims=True) + epsilon)
        scale = scale_rows[pl.ds(level, 1), :]
        shift = shift_rows[pl.ds(level, 1), :]
        hidden[pl.ds(f * tok, tok), :] = x * inverse * (1.0 + scale) + shift
    for c in range(parts):
        gathered[c, me] = hidden[:, c * cw : (c + 1) * cw].astype(BF16)
    raw[...] = jnp.zeros_like(raw)
    hand[...] = jnp.zeros_like(hand)
    pl.semaphore_wait(barrier, 2 * n - 1)

    def ag_copy(c, zb, yb, kind, to):
        ref = gathered.at[c, zb * 2 + yb]
        return remote(ref, ref, ag_send.at[c, zb, kind], ag_recv.at[c, zb * 2 + yb], to, seg)

    def ag_forward(d, c, act):
        up, down = z - d, z + d
        if d > 0:
            @pl.when(up >= 0)
            def _():
                if act == "start":
                    ag_copy(c, up, y, 2, me).wait_recv()
                move(ag_copy(c, up, y, 2, z * 2 + 1 - y), act)

        @pl.when((up >= 0) & (z + 1 < nz))
        def _():
            move(ag_copy(c, up, y, 0, me + 2), act)

        @pl.when(down < nz)
        def _():
            if d > 0 and act == "start":
                ag_copy(c, down, y, 2, me).wait_recv()
            move(ag_copy(c, down, y, 2, z * 2 + 1 - y), act)

        @pl.when((down < nz) & (z > 0))
        def _():
            move(ag_copy(c, down, y, 1, me - 2), act)

    def move(copy, act):
        if act == "start":
            copy.start()
        else:
            copy.wait_send()

    for d in range(nz - 1):
        @pl.loop(0, parts)
        def _(c):
            ag_forward(d, c, "start")

    for copy in locals_[2:5]:
        copy.wait()

    @pl.loop(0, parts + 1)
    def _(t):
        @pl.when(t < parts)
        def _():
            ag_forward(nz - 1, t, "start")

        @pl.when(t > 0)
        def _():
            c = t - 1

            @pl.loop(0, nz)
            def _(zb):
                ag_copy(c, zb, 1 - y, 2, me).wait_recv()

            at = pl.multiple_of(c * cw, cw)
            raw[...] += jnp.dot(
                gathered[c].reshape(rows, cw), w_in[pl.ds(at, cw), :],
                preferred_element_type=F32,
            )

    ones = jnp.ones((8, lw), F32)
    q_raw = raw[:, :lw]
    k_raw = raw[:, lw : 2 * lw]
    q_sq = lax.dot_general(ones, q_raw * q_raw, NT, precision=lax.Precision.HIGHEST,
                           preferred_element_type=F32)
    k_sq = lax.dot_general(ones, k_raw * k_raw, NT, precision=lax.Precision.HIGHEST,
                           preferred_element_type=F32)
    row_id = lax.broadcasted_iota(jnp.int32, (8, rows), 0)
    stats[seg, me] = jnp.where(row_id == 0, q_sq, k_sq)

    def st_copy(slot, to):
        s, g = quotient(to, 2), remainder(to, 2)
        ref = stats.at[seg, me]
        return remote(ref, ref, st_send.at[slot], st_recv.at[seg, me], s, g)

    @pl.loop(1, 2 * n)
    def _(k):
        st_copy(k, remainder(me * 2 + seg + k, 2 * n)).start()

    keys[seg] = (k_raw * kgain_ref[...]).astype(BF16)
    vals[seg] = raw[:, 2 * lw :].astype(BF16)
    k_copy = remote(keys.at[seg], keys.at[seg], kv_send.at[0], kv_recv.at[0], me, other)
    v_copy = remote(vals.at[seg], vals.at[seg], kv_send.at[1], kv_recv.at[1], me, other)
    k_copy.start()
    v_copy.start()

    for d in range(nz):
        @pl.loop(0, parts)
        def _(c):
            ag_forward(d, c, "drain")

    @pl.loop(1, 2 * n)
    def _(k):
        peer = remainder(me * 2 + seg + k, 2 * n)
        ref = stats.at[remainder(peer, 2), quotient(peer, 2)]
        remote(ref, ref, st_send.at[k],
               st_recv.at[remainder(peer, 2), quotient(peer, 2)], me, other).wait_recv()

    inner = n * lw
    totals = lax.rsqrt(jnp.sum(stats[...], axis=1) / inner + epsilon)
    own_totals = jnp.where(seg == 0, totals[0], totals[1])
    q_inverse = jnp.transpose(own_totals)[:, 0:1]
    queries = (raw[:, :lw] * q_inverse * qgain_ref[...]).astype(BF16)
    raw[:, :lw] = queries.astype(F32)
    k_inverse = jnp.concatenate([totals[0, 1:2], totals[1, 1:2]], axis=1) * HD ** (-0.5)
    k_copy.wait_recv()
    v_copy.wait_recv()

    qb = min(rows, 256)
    key_id = lax.broadcasted_iota(jnp.int32, (qb, 2 * rows), 1)
    key_frame = quotient(key_id, rows) * frames + quotient(remainder(key_id, block), tok)
    query_id = lax.broadcasted_iota(jnp.int32, (qb, 1), 0)
    query_frame = quotient(remainder(query_id, block), tok)
    begin = jnp.zeros((qb, 1), jnp.int32)
    for f in range(frames):
        begin = jnp.where(query_frame == f, seg * frames + f - start_ref[f], begin)
    usable = (key_frame >= begin) & (key_frame < begin + KEYWIN)

    @pl.loop(0, rows // qb)
    def _(b):
        at = pl.ds(pl.multiple_of(b * qb, qb), qb)
        for h in range(heads):
            lanes = slice(h * HD, (h + 1) * HD)
            head_keys = keys[:, :, lanes].reshape(2 * rows, HD)
            head_vals = vals[:, :, lanes].reshape(2 * rows, HD)
            scores = lax.dot_general(raw[at, lanes].astype(BF16), head_keys, NT,
                                     preferred_element_type=F32) * k_inverse
            scores = jnp.where(usable, scores, masked_score)
            lifted = jnp.exp(scores - jnp.max(scores, axis=1, keepdims=True))
            weights = (lifted / jnp.sum(lifted, axis=1, keepdims=True)).astype(BF16)
            att[at, lanes] = jnp.dot(weights, head_vals, preferred_element_type=F32).astype(BF16)

    def y_copy(c):
        return remote(partial.at[c, 1 - y], from_y.at[c], y_send.at[c], y_recv.at[c],
                      z * 2 + 1 - y, seg)

    for c in range(parts):
        wo_copies[c].wait()
        product = jnp.dot(att[...], w_out[c], preferred_element_type=F32).astype(BF16)
        product = product.reshape(nz, 2, block, cw)
        partial[c, 0] = product[:, 0]
        partial[c, 1] = product[:, 1]
        y_copy(c).start()

    def up_copy(c, zb):
        return remote(partial.at[c, y, zb], from_up.at[c, zb], z_send.at[c, zb],
                      up_recv.at[c, zb], me + 2, seg)

    def down_copy(c, zb):
        return remote(partial.at[c, y, zb], from_down.at[c, zb], z_send.at[c, zb],
                      down_recv.at[c, zb], me - 2, seg)

    def add(c, zb, other_ref):
        total = partial[c, y, zb].astype(F32) + other_ref[c, zb].astype(F32)
        partial[c, y, zb] = total.astype(BF16)

    @pl.loop(0, parts + nz - 1)
    def _(t):
        @pl.when(t < parts)
        def _():
            y_copy(t).wait_recv()

            @pl.loop(0, nz)
            def _(zb):
                add(t, zb, from_y)

        up, down = t - z, t - (nz - 1 - z)

        @pl.when((up >= 0) & (up < parts) & (z + 1 < nz))
        def _():
            @pl.loop(z + 1, nz)
            def _(zb):
                @pl.when(z > 0)
                def _():
                    up_copy(up, zb).wait_recv()
                    add(up, zb, from_up)

                up_copy(up, zb).start()

        @pl.when((down >= 0) & (down < parts) & (z > 0))
        def _():
            @pl.loop(0, z)
            def _(zb):
                @pl.when(z + 1 < nz)
                def _():
                    down_copy(down, zb).wait_recv()
                    add(down, zb, from_down)

                down_copy(down, zb).start()

        @pl.when(t >= nz - 1)
        def _():
            c = t - (nz - 1)
            projected[c] = partial[c, y, z].astype(F32)

            @pl.when(z > 0)
            def _():
                up_copy(c, z).wait_recv()
                projected[c] += from_up[c, z].astype(F32)

            @pl.when(z + 1 < nz)
            def _():
                down_copy(c, z).wait_recv()
                projected[c] += from_down[c, z].astype(F32)

    locals_[5].wait()
    hand_copy = remote(hand.at[0], hand.at[1], hand_send, hand_recv, me, 0)
    for f in range(frames):
        gate = gate_rows[pl.ds(level_ref[f], 1), :]
        for c in range(parts):
            lanes = slice(c * cw, (c + 1) * cw)
            updated = x_ref[f, :, lanes].astype(F32) + (
                gate[:, lanes] * projected[c, f * tok : (f + 1) * tok, :]
            )
            updated = updated.astype(BF16)
            if f == 0:
                departed_ref[0, 0, :, lanes] = updated
                hand[0, 0:tok, lanes] = updated
            else:
                queue_ref[f - 1, :, lanes] = updated
        if f == 0:
            @pl.when(seg == 1)
            def _():
                hand_copy.start()

    @pl.loop(0, parts)
    def _(c):
        y_copy(c).wait_send()

        @pl.loop(z + 1, nz)
        def _(zb):
            up_copy(c, zb).wait_send()

        @pl.loop(0, z)
        def _(zb):
            down_copy(c, zb).wait_send()

    @pl.loop(1, 2 * n)
    def _(k):
        st_copy(k, remainder(me * 2 + seg + k, 2 * n)).wait_send()

    k_copy.wait_send()
    v_copy.wait_send()

    @pl.when(seg == 1)
    def _():
        queue_ref[frames - 1] = fresh_ref[0]
        hand_copy.wait_send()

    @pl.when(seg == 0)
    def _():
        hand_copy.wait_recv()
        queue_ref[frames - 1] = hand[1, 0:tok, :]


def shards(
    n, queue_frames, fresh_frames, slot_level, window_start, shift_table, scale_table, gate_table,
    w_query, w_key, w_value, w_out, query_gain, key_gain,
):
    frames, tok, width = queue_frames.shape
    parts = chunk_count(width)
    cw = width // parts
    block = frames * tok
    rows = n * block
    lw = w_query.shape[1]
    nz = n // 2
    levels = shift_table.shape[0]
    vmem = pl.BlockSpec(memory_space=pltpu.VMEM)
    smem = pl.BlockSpec(memory_space=pltpu.SMEM)
    hbm = pl.BlockSpec(memory_space=pl.ANY)
    dma = pltpu.SemaphoreType.DMA
    scratch = [
        pltpu.VMEM((levels, width), F32),
        pltpu.VMEM((levels, width), F32),
        pltpu.VMEM((levels, width), F32),
        pltpu.VMEM((width, 3 * lw), BF16),
        pltpu.VMEM((parts, lw, cw), BF16),
        pltpu.VMEM((block, width), F32),
        pltpu.VMEM((parts, n, block, cw), BF16),
        pltpu.VMEM((rows, 3 * lw), F32),
        pltpu.VMEM((2, n, 8, rows), F32),
        pltpu.VMEM((2, rows, lw), BF16),
        pltpu.VMEM((2, rows, lw), BF16),
        pltpu.VMEM((rows, lw), BF16),
        pltpu.VMEM((parts, 2, nz, block, cw), BF16),
        pltpu.VMEM((parts, nz, block, cw), BF16),
        pltpu.VMEM((parts, nz, block, cw), BF16),
        pltpu.VMEM((parts, nz, block, cw), BF16),
        pltpu.VMEM((parts, block, cw), F32),
        pltpu.VMEM((2, 16, width), BF16),
        dma((6,)),
        dma((parts,)),
        dma((parts, nz, 3)),
        dma((parts, n)),
        dma((2 * n,)),
        dma((2, n)),
        dma((2,)),
        dma((2,)),
        dma((parts,)),
        dma((parts,)),
        dma((parts, nz)),
        dma((parts, nz)),
        dma((parts, nz)),
        dma,
        dma,
    ]
    return pl.pallas_call(
        functools.partial(kernel, n, frames, tok, parts),
        out_shape=(
            jax.ShapeDtypeStruct((frames, tok, width), BF16),
            jax.ShapeDtypeStruct((1, 1, tok, width), BF16),
        ),
        in_specs=[vmem, vmem, smem, smem] + [hbm] * 7 + [vmem, vmem],
        out_specs=(vmem, vmem),
        scratch_shapes=scratch,
        compiler_params=pltpu.CompilerParams(
            collective_id=0, has_side_effects=True, vmem_limit_bytes=60 * 1024 * 1024
        ),
    )(
        queue_frames, fresh_frames, slot_level, window_start, shift_table, scale_table, gate_table,
        w_query, w_key, w_value, w_out, query_gain[None], key_gain[None],
    )


def solution(mesh):
    n = mesh.shape["seq"]
    assert n % 2 == 0 and mesh.shape["segment"] == 2
    return jax.shard_map(
        functools.partial(shards, n),
        mesh=mesh,
        in_specs=(
            P(("groups", "segment"), "seq", None),
            P("groups", "seq", None),
            P(("groups", "segment")),
            P(("groups", "segment")),
            P(),
            P(),
            P(),
            P(None, "seq"),
            P(None, "seq"),
            P(None, "seq"),
            P("seq", None),
            P("seq"),
            P("seq"),
        ),
        out_specs=(
            P(("groups", "segment"), "seq", None),
            P(("groups", "segment"), None, "seq", None),
        ),
        check_vma=False,
    )
```

time: 200 us -> 101 us (0.51)
  waiting for transfers between devices: 128 us -> 0 us
  Pallas kernels: 0 us -> 97.3 us
  matrix products: 21.3 us -> 0 us
  blocking collectives: 19.3 us -> 0 us
  between operations: 14.3 us -> 0.64 us
  other arithmetic: 6.01 us -> 0 us
  local copies, waits for them, and re-layouts: 7.4 us -> 3.22 us
  starting transfers between devices: 3.97 us -> 0 us
    pallas_call x0 -> x1, Pallas kernels: none -> 97.3 us  [shards(): pl.pallas_call(functools.partial(kernel, n, frames, tok, parts), out_shap...]
    reduce_scatter x1 -> x0, waiting for transfers between devices: 67.5 us -> none  [shards(): lax.psum_scatter(partial_value.astype(jnp.float32).astype(jnp.bfloat16),...]
    all_gather x1 -> x0, waiting for transfers between devices: 56.8 us -> none  [shards(): lax.all_gather(hidden, 'seq', axis=1, tiled=True)]
    dot_general x7 -> x0, matrix products: 21.3 us -> none  [the longest x1 8.56 us: shards(): jnp.einsum('ftd,de->fte', lax.all_gather(hidden, 'seq', axis=1, tiled=Tru...]
    psum x1 -> x0, blocking collectives: 19.3 us -> none  [shards(): lax.psum((jnp.sum(q_raw * q_raw, axis=2), jnp.sum(k_raw * k_raw, axis=2))...]
    ppermute x3 -> x0, starting transfers between devices: 3.89 us -> none  [the longest x1 1.3 us: extended(): before = lax.ppermute(last, axis, up)]
    ppermute x3 -> x0, waiting for transfers between devices: 3.52 us -> none  [the longest x1 1.79 us: extended(): after = lax.ppermute(leading, axis, down)]
    convert_element_type x2 -> x0, other arithmetic: 2.97 us -> none  [the longest x1 1.88 us: shards(): hidden = (values_in * inverse[:, :, None] * (1.0 + scale_rows[:, None]) +...]
  transfers between devices with their start and end apart: 5 -> 0, of which waited for: 4 -> 0; matrix products, arithmetic and copies ran while one was open for 1% -> 0% of each run, Pallas kernels for 0% -> 0%
where the time goes in v1:
time: 101 us
  Pallas kernels  97.3 us (96%)
  local copies, waits for them, and re-layouts  3.22 us (3%)
    pallas_call x1, Pallas kernels, shards(): pl.pallas_call(functools.partial(kernel, n, frames, tok, parts), out_shap...  97.3 us
    unnamed x2, local copies, waits for them, and re-layouts  3.22 us

profile of v1, /device:TPU:0, one launch (start us, length us, event | category | flops | bytes accessed | tf_op | source)
XLA Modules:
  0.0 101.1 jit_solution(14649552166994347501)
XLA Ops:
  0.6 97.3 %shard_map.140 = (bf16[8,4,5120]{2,1,0:T(4,128)(2,1)}, bf16[1,1,4,5120]{3,2,1,0:T(4,128)(2,1)}) custom-call(bf16[8,4,5120]{2,1,0:T(4,128)(2,1)} %x_ref.1, bf16[1,4,5120]{2,1,0:T(4,128)(2,1)} %fresh_ref.1, s32[8]{0:T(128)} %level_ref.1, s32[8]{0:T(128)} %start_ref.1, f32[50,5120]{1,0:T(8,128)} %shift_hbm.1, f32[50,5120]{1,0:T(8,128)} %scale_hbm.1, ...), custom_call_target="tpu_custom_call" | custom-call | tf_op jit(solution)/shard_map/pallas_call | solution.py:412
  97.9 1.8 %copy.17 = bf16[8,4,5120]{2,1,0:T(4,128)(2,1)} copy(bf16[8,4,5120]{2,1,0:T(4,128)(2,1)} %get-tuple-element.4) | data formatting | bytes 655360
  99.7 1.4 %copy.18 = bf16[1,1,4,5120]{3,2,1,0:T(4,128)(2,1)} copy(bf16[1,1,4,5120]{3,2,1,0:T(4,128)(2,1)} %get-tuple-element.5) | data formatting | bytes 81920
